TPU v7x, 256 devices: a whole 4x4x8 slice. The times are simulated.
256 devices in a mesh: group: 8 (over z), block: 32 (over x, y, core).
Axes of the slice: x: 4, y: 4, z: 8, core: 2. Of those that a mesh axis runs over, the one named last changes fastest.
Arguments:
- jacobians: bfloat16 [3072, 128, 1152], P(('group', 'block')), may hold values from -0.15625 to 0.15625
- destination: int32 [3072], P(('group', 'block')), may hold values from 0 to 31, as said below
- other_group: int32 [3072], P(('group', 'block')), may hold values from 0 to 7, as said below
- live_rows: int32 [3072], P(('group', 'block')), may hold values from 64 to 128, as said below
- damping: float32 [256, 576], P(('group', 'block')), may hold values from 0.5 to 2
- right_side: float32 [256, 576], P(('group', 'block')), may hold values from -18 to 18
Outputs:
- solution: float32 [256, 576], P(('group', 'block'))
- residual: float32 [256, 576], P(('group', 'block'))
Inputs may be any that keep to these rules, and one draw needn't show every extreme that they name: `destination`: the observation blocks of one device name any one camera block at most 2 times; in every group some camera block is named exactly 2 times by every device of that group. `other_group`: an observation block's covisible group differs from the group of the device that holds it. `live_rows`: every device holds a block whose 128 rows are all live.
All inputs are finite; a program needn't handle non-finite values.
Results may differ from a plain program's by a relative error of at most 0.009.
Values may be sent and summed in bfloat16 or wider, within the bound.
A program may use at most 128 MiB of HBM per device.

v0:
```python
import jax
import jax.numpy as jnp
from jax import lax
from jax.sharding import PartitionSpec as P

ITERS = 2


def global_norm(residual, scaled_res):
    return lax.psum(jnp.sum(residual * scaled_res), ("group", "block"))


def on_device(jacobians, destination, other_group, live_rows, damping, right_side):
    block_count, row_count, block_width = jacobians.shape
    param_count = block_width // 2
    owners = lax.axis_size("block")
    groups = lax.axis_size("group")
    my_group = lax.axis_index("group")
    row_index = jnp.arange(row_count, dtype=jnp.int32)
    kept_blocks = jnp.where(
        row_index[None, :, None] < live_rows[:, None, None], jacobians, jnp.zeros_like(jacobians)
    )
    capacity = max(2, 2 * ((block_count + owners - 1) // owners))
    same_owner = destination[:, None] == destination[None, :]
    positions = jnp.arange(block_count, dtype=jnp.int32)
    before = positions[None, :] < positions[:, None]
    slot_rank = jnp.sum((same_owner & before).astype(jnp.int32), axis=1)
    slot_index = destination * capacity + slot_rank
    send_blocks = (
        jnp.zeros((owners * capacity, row_count, block_width), jnp.bfloat16)
        .at[slot_index]
        .set(kept_blocks)
    )
    send_groups = jnp.zeros((owners * capacity,), jnp.int32).at[slot_index].set(other_group)
    send_blocks = send_blocks.reshape(owners, capacity, row_count, block_width)
    send_groups = send_groups.reshape(owners, capacity)
    got_blocks, got_groups = (
        lax.all_to_all(send_blocks, "block", split_axis=0, concat_axis=0, tiled=True),
        lax.all_to_all(send_groups, "block", split_axis=0, concat_axis=0, tiled=True),
    )
    got_blocks = got_blocks.reshape(owners * capacity, row_count, block_width)
    got_groups = got_groups.reshape(owners * capacity)
    group_ids = jnp.arange(groups, dtype=jnp.int32)
    own_mask = (group_ids == my_group).astype(jnp.float32)
    selector = (got_groups[:, None] == group_ids[None, :]).astype(jnp.float32)
    selector_low = selector.astype(jnp.bfloat16)

    def spread(term_rows):
        home_total = jnp.sum(term_rows[:, :param_count], axis=0)
        far_total = jnp.dot(
            selector.T,
            term_rows[:, param_count:],
            precision=lax.Precision.HIGHEST,
            preferred_element_type=jnp.float32,
        )
        return far_total + own_mask[:, None] * home_total[None, :]

    squares = jnp.einsum("src,src->sc", got_blocks, got_blocks, preferred_element_type=jnp.float32)
    diagonal_sum = damping + lax.psum_scatter(
        spread(squares), "group", scatter_dimension=0, tiled=True
    )
    solution = jnp.zeros_like(right_side)
    residual = right_side
    scaled_res = residual / diagonal_sum
    direction = scaled_res
    precond_norm = global_norm(residual, scaled_res)
    for iteration in range(ITERS):
        low_field = direction.astype(jnp.bfloat16)
        panel_low = lax.all_gather(low_field, "group", axis=0, tiled=True)
        far_inputs = jnp.dot(selector_low, panel_low, preferred_element_type=jnp.float32).astype(
            jnp.bfloat16
        )
        near_inputs = jnp.broadcast_to(low_field, far_inputs.shape)
        inputs = jnp.concatenate([near_inputs, far_inputs], axis=1)
        projected = jnp.einsum(
            "src,sc->sr", got_blocks, inputs, preferred_element_type=jnp.float32
        ).astype(jnp.bfloat16)
        returned = jnp.einsum(
            "src,sr->sc", got_blocks, projected, preferred_element_type=jnp.float32
        )
        operator_image = damping * direction + lax.psum_scatter(
            spread(returned), "group", scatter_dimension=0, tiled=True
        )
        curvature = lax.psum(jnp.sum(direction * operator_image), ("group", "block"))
        step_size = precond_norm / curvature
        solution = solution + step_size * direction
        residual = residual - step_size * operator_image
        if iteration + 1 < ITERS:
            scaled_res = residual / diagonal_sum
            next_norm = global_norm(residual, scaled_res)
            direction = scaled_res + next_norm / precond_norm * direction
            precond_norm = next_norm
    return (solution, residual)


def solution(mesh):
    placed = (
        P(("group", "block"), None, None),
        P(("group", "block")),
        P(("group", "block")),
        P(("group", "block")),
        P(("group", "block"), None),
        P(("group", "block"), None),
    )
    return jax.shard_map(
        on_device,
        mesh=mesh,
        in_specs=placed,
        out_specs=(P(("group", "block"), None), P(("group", "block"), None)),
        check_vma=False,
    )
```

profile of v0, /device:TPU:1, one launch (start us, length us, event | category | flops | bytes accessed | tf_op | source)
XLA Modules:
  0.0 751.9 jit_solution(11086218036957085777)
XLA Ops:
  0.6 0.9 convert_reduce_fusion
  1.5 0.7 compare_select_fusion
  2.2 0.7 scatter_custom_fusion
  3.0 0.7 all_to_all.9
  3.7 8.6 %all-to-all-start = ((s32[32,1,2]{2,1,0:T(1,128)}), s32[32,1,2]{2,1,0:T(1,128)S(1)}, u32[]{:S(2)}, u32[]{:S(2)}) async-start(s32[32,1,2]{2,1,0:T(1,128)} %bitcast.2), calls=%async_computation | async-start | bytes 32768 | tf_op jit(solution)/shard_map/all_to_all | solution.py:39
  12.3 0.7 iota_compare_fusion.4
  13.0 2.3 broadcast_select_fusion
  15.3 7.1 broadcast_in_dim.26
  22.4 7.7 %scatter_fusion = bf16[64,128,1152]{2,1,0:T(8,128)(2,1)} fusion(bf16[64,128,1152]{2,1,0:T(8,128)(2,1)} %broadcast_in_dim.26, s32[12]{0:T(128)} %copy-done.2, bf16[12,128,1152]{2,1,0:T(8,128)(2,1)S(1)} %broadcast_select_fusion), kind=kCustom, calls=%fused_computation.1 | custom fusion | bytes 10616880 | tf_op jit(solution)/shard_map/scatter | solution.py:32
  30.2 7.5 %all-to-all-start.1 = ((bf16[32,2,128,1152]{3,2,1,0:T(8,128)(2,1)}), bf16[32,2,128,1152]{3,2,1,0:T(8,128)(2,1)}, u32[]{:S(2)}, u32[]{:S(2)}) async-start(bf16[32,2,128,1152]{3,2,1,0:T(8,128)(2,1)} %bitcast.41), calls=%async_computation.1 | async-start | bytes 37748736 | tf_op jit(solution)/shard_map/all_to_all | solution.py:38
  37.7 0.6 dynamic-slice
  38.3 0.5 broadcast.51
  38.8 0.7 reduce.9
  39.6 261.2 %all-to-all-done.1 = bf16[32,2,128,1152]{3,2,1,0:T(8,128)(2,1)} async-done(((bf16[32,2,128,1152]{3,2,1,0:T(8,128)(2,1)}), bf16[32,2,128,1152]{3,2,1,0:T(8,128)(2,1)}, u32[]{:S(2)}, u32[]{:S(2)}) %all-to-all-start.1) | async-done | bytes 18874400 | tf_op jit(solution)/shard_map/all_to_all | solution.py:38
  300.8 8.3 %fusion = f32[64,1152]{1,0:T(8,128)S(1)} fusion(bf16[32,2,128,1152]{3,2,1,0:T(8,128)(2,1)} %all-to-all-done.1), kind=kLoop, calls=%fused_computation.3 | loop fusion | flops 28237824 | bytes 19169280 | tf_op jit(solution)/shard_map/src,src->sc/dot_general | solution.py:58
  309.4 25.5 %all-reduce = f32[8,576]{1,0:T(8,128)S(1)} all-reduce(f32[8,576]{1,0:T(8,128)S(1)} %convolution_add_fusion.2), channel_id=2, replica_groups=mesh['group'=8,'block'=32] {'group'}, use_global_device_ids=true, to_apply=%region_4.5.clone | all-reduce | flops 4608 | bytes 36864
  334.9 0.7 convert_reduce_fusion.2
  335.6 18.1 %all-gather = bf16[8,1,576]{2,1,0:T(2,128)(2,1)S(1)} all-gather(bf16[1,1,576]{2,1,0:T(2,128)(2,1)S(1)} %convert_bitcast_fusion.3), channel_id=1, replica_groups=mesh['group'=8,'block'=32] {'group'}, dimensions={0}, use_global_device_ids=true | all-gather | bytes 10368 | tf_op jit(solution)/shard_map/all_gather | solution.py:69
  354.0 10.1 %fusion.3 = f32[64,1,128]{2,1,0:T(1,128)S(1)} fusion(bf16[64,128,1152]{2,1,0:T(8,128)(2,1)} %bitcast.4, bf16[64,1152,1]{1,0,2:T(8,128)(2,1)S(1)} %maximum_bitcast_fusion), kind=kOutput, calls=%fused_computation.14 | convolution fusion | flops 18874368 | bytes 19054592 | tf_op jit(solution)/shard_map/src,sc->sr/dot_general | solution.py:75
  364.2 7.8 %fusion.10 = f32[64,1,1152]{2,1,0:T(1,128)S(1)} fusion(bf16[64,128,1152]{2,1,0:T(8,128)(2,1)} %bitcast.4, bf16[64,128,1]{1,0,2:T(8,128)(2,1)S(1)} %convert_bitcast_fusion.1), kind=kOutput, calls=%fused_computation.26 | convolution fusion | flops 18874368 | bytes 19185664 | tf_op jit(solution)/shard_map/src,sr->sc/dot_general | solution.py:78
  372.4 20.1 %all-reduce.1 = f32[8,576]{1,0:T(8,128)S(1)} all-reduce(f32[8,576]{1,0:T(8,128)S(1)} %convolution_add_fusion.1), channel_id=3, replica_groups=mesh['group'=8,'block'=32] {'group'}, use_global_device_ids=true, to_apply=%region_8.9.clone | all-reduce | flops 4608 | bytes 36864
  392.5 1.2 multiply_reduce_fusion.2
  393.7 133.7 %all-reduce.3 = (f32[]{:T(128)}, f32[]{:T(128)}) all-reduce(f32[]{:T(128)} %get-tuple-element.3, f32[]{:T(128)} %get-tuple-element.2), channel_id=1, replica_groups=mesh['group'=8,'block'=32] {'group','block'}, use_global_device_ids=true, to_apply=%region_6.7 | all-reduce | flops 2 | bytes 16 | tf_op jit(solution)/shard_map/psum | solution.py:10
  528.7 1.2 multiply_reduce_fusion.1
  530.0 73.4 %psum.30 = f32[]{:T(128)} all-reduce(f32[]{:T(128)} %get-tuple-element.8), channel_id=1, replica_groups=mesh['group'=8,'block'=32] {'group','block'}, use_global_device_ids=true, to_apply=%region_12.13 | all-reduce | flops 1 | bytes 8 | tf_op jit(solution)/shard_map/psum | solution.py:10
  604.8 17.9 %all-gather.1 = bf16[8,1,576]{2,1,0:T(2,128)(2,1)S(1)} all-gather(bf16[1,1,576]{2,1,0:T(2,128)(2,1)S(1)} %convert_bitcast_fusion.2), channel_id=1, replica_groups=mesh['group'=8,'block'=32] {'group'}, dimensions={0}, use_global_device_ids=true | all-gather | bytes 10368 | tf_op jit(solution)/shard_map/all_gather | solution.py:69
  623.0 10.1 %fusion.1 = f32[64,1,128]{2,1,0:T(1,128)S(1)} fusion(bf16[64,128,1152]{2,1,0:T(8,128)(2,1)} %bitcast.4, bf16[64,1152,1]{1,0,2:T(8,128)(2,1)S(1)} %maximum_bitcast_fusion.1), kind=kOutput, calls=%fused_computation.11 | convolution fusion | flops 18874368 | bytes 19054592 | tf_op jit(solution)/shard_map/src,sc->sr/dot_general | solution.py:75
  633.2 7.8 %fusion.8 = f32[64,1,1152]{2,1,0:T(1,128)S(1)} fusion(bf16[64,128,1152]{2,1,0:T(8,128)(2,1)} %bitcast.4, bf16[64,128,1]{1,0,2:T(8,128)(2,1)S(1)} %convert_bitcast_fusion), kind=kOutput, calls=%fused_computation.24 | convolution fusion | flops 18874368 | bytes 19185664 | tf_op jit(solution)/shard_map/src,sr->sc/dot_general | solution.py:78
  641.4 20.9 %all-reduce.2 = f32[8,576]{1,0:T(8,128)S(1)} all-reduce(f32[8,576]{1,0:T(8,128)S(1)} %convolution_add_fusion), channel_id=4, replica_groups=mesh['group'=8,'block'=32] {'group'}, use_global_device_ids=true, to_apply=%region_14.15.clone | all-reduce | flops 4608 | bytes 36864
  662.3 1.2 multiply_reduce_fusion
  663.5 85.8 %psum.31 = f32[]{:T(128)} all-reduce(f32[]{:T(128)} %multiply_reduce_fusion), channel_id=1, replica_groups=mesh['group'=8,'block'=32] {'group','block'}, use_global_device_ids=true, to_apply=%region_16.17 | all-reduce | flops 1 | bytes 8 | tf_op jit(solution)/shard_map/psum | solution.py:84
  750.7 1.2 multiply_subtract_fusion
  (30 shorter events, 1.8 us)
Async XLA Ops:
  2.2 10.0 %copy-start.2 = (s32[12]{0:T(128)}, s32[12]{0:T(128)S(1)}, u32[]{:S(2)}) copy-start(s32[12]{0:T(128)S(1)} %compare_select_fusion) | copy-start | bytes 148
  3.7 26.5 %all-to-all-start = ((s32[32,1,2]{2,1,0:T(1,128)}), s32[32,1,2]{2,1,0:T(1,128)S(1)}, u32[]{:S(2)}, u32[]{:S(2)}) async-start(s32[32,1,2]{2,1,0:T(1,128)} %bitcast.2), calls=%async_computation | async-start | bytes 32768 | tf_op jit(solution)/shard_map/all_to_all | solution.py:39
  30.2 7.6 %copy-start.3 = (u32[256]{0:T(256)S(1)}, u32[256]{0:T(256)}, u32[]{:S(2)}) copy-start(u32[256]{0:T(256)} %constant.28) | copy-start | bytes 3076
  30.2 270.6 %all-to-all-start.1 = ((bf16[32,2,128,1152]{3,2,1,0:T(8,128)(2,1)}), bf16[32,2,128,1152]{3,2,1,0:T(8,128)(2,1)}, u32[]{:S(2)}, u32[]{:S(2)}) async-start(bf16[32,2,128,1152]{3,2,1,0:T(8,128)(2,1)} %bitcast.41), calls=%async_computation.1 | async-start | bytes 37748736 | tf_op jit(solution)/shard_map/all_to_all | solution.py:38
  37.7 297.2 %copy-start = (f32[1,576]{1,0:T(1,128)S(1)}, f32[1,576]{1,0:T(1,128)}, u32[]{:S(2)}) copy-start(f32[1,576]{1,0:T(1,128)} %param.10) | copy-start | bytes 6916
  37.7 297.2 %copy-start.1 = (f32[1,576]{1,0:T(1,128)S(1)}, f32[1,576]{1,0:T(1,128)}, u32[]{:S(2)}) copy-start(f32[1,576]{1,0:T(1,128)} %param.11) | copy-start | bytes 6916
where the time goes:
time: 753 us; the launch traced here: 752 us
  blocking collectives  396 us (53%)
  waiting for transfers between devices  261 us (35%)
  matrix products  37.2 us (5%)
  other arithmetic  19.4 us (3%)
  local copies, waits for them, and re-layouts  17.6 us (2%)
  starting transfers between devices  16.1 us (2%)
    all_to_all x1, waiting for transfers between devices, on_device(): lax.all_to_all(send_blocks, 'block', split_axis=0, concat_axis=0, tiled=T...  261 us
    psum x2, blocking collectives, global_norm(): return lax.psum(jnp.sum(residual * scaled_res), ('group', 'block'))  207 us
    psum x1, blocking collectives, on_device(): lax.psum(jnp.sum(direction * operator_image), ('group', 'block'))  85.8 us
    unnamed x3, blocking collectives  66.6 us
    all_gather x2, blocking collectives, on_device(): panel_low = lax.all_gather(low_field, 'group', axis=0, tiled=True)  36.1 us
    dot_general x2, matrix products, on_device(): jnp.einsum('src,sc->sr', got_blocks, inputs, preferred_element_type=jnp.f...  20.3 us
    dot_general x2, matrix products, on_device(): jnp.einsum('src,sr->sc', got_blocks, projected, preferred_element_type=jn...  15.7 us
  transfers between devices with their start and end apart: 2, of which 1 were waited for; matrix products, arithmetic and copies ran while one was open for 3% of the time, Pallas kernels for 0%

commit v1 on v0

--- a/solution.py
+++ b/solution.py
@@ -2,6 +2,7 @@
 import jax.numpy as jnp
 from jax import lax
 from jax.sharding import PartitionSpec as P
+from jax.lax import axis_index, axis_size, ppermute
 
 ITERS = 2
 
@@ -66,7 +67,22 @@
     precond_norm = global_norm(residual, scaled_res)
     for iteration in range(ITERS):
         low_field = direction.astype(jnp.bfloat16)
-        panel_low = lax.all_gather(low_field, "group", axis=0, tiled=True)
+        n_shards = axis_size("group")
+        heap = []
+        for q in [*range(n_shards)]:
+            heap.append((q, (q + 1) % n_shards))
+        gallery = []
+        for q in tuple(range(n_shards)):
+            gallery.append((q, (q - 1) % n_shards))
+        p_next, v_next = ([low_field], [low_field])
+        for _ in range(n_shards // 2):
+            p_next.append(ppermute(p_next[-1], axis_name="group", perm=heap))
+        for _ in tuple(range((n_shards - 1) // 2)):
+            v_next.append(ppermute(v_next[-1], axis_name="group", perm=gallery))
+        r_now = jnp.concatenate([*p_next[::-1], *v_next[1:]], 0)
+        panel_low = jnp.roll(
+            r_now, (axis_index("group") - n_shards // 2) * low_field.shape[0], axis=0
+        )
         far_inputs = jnp.dot(selector_low, panel_low, preferred_element_type=jnp.float32).astype(
             jnp.bfloat16
         )

time: 753 us -> 742 us (0.985)
  blocking collectives: 396 us -> 355 us
  starting transfers between devices: 16.1 us -> 32.3 us
  waiting for transfers between devices: 261 us -> 274 us
    all_gather x2 -> x0, blocking collectives: 36.1 us -> none  [on_device(): panel_low = lax.all_gather(low_field, 'group', axis=0, tiled=True)]
    ppermute x0 -> x14, starting transfers between devices: none -> 16.2 us  [the longest x6 15.1 us: on_device(): v_next.append(ppermute(v_next[-1], axis_name='group', perm=gallery))]
    ppermute x0 -> x14, waiting for transfers between devices: none -> 13.2 us  [the longest x8 13.2 us: on_device(): p_next.append(ppermute(p_next[-1], axis_name='group', perm=heap))]
  transfers between devices with their start and end apart: 2 -> 16, of which waited for: 1 -> 9; matrix products, arithmetic and copies ran while one was open for 3% -> 3% of each run, Pallas kernels for 0% -> 0%
where the time goes in v1:
time: 742 us; the launch traced here: 741 us
  blocking collectives  355 us (48%)
  waiting for transfers between devices  274 us (37%)
  matrix products  37.2 us (5%)
  starting transfers between devices  32.3 us (4%)
  other arithmetic  19.4 us (3%)
  local copies, waits for them, and re-layouts  17.7 us (2%)
    all_to_all x1, waiting for transfers between devices, on_device(): lax.all_to_all(send_blocks, 'block', split_axis=0, concat_axis=0, tiled=T...  261 us
    psum x2, blocking collectives, global_norm(): return lax.psum(jnp.sum(residual * scaled_res), ('group', 'block'))  206 us
    psum x1, blocking collectives, on_device(): lax.psum(jnp.sum(direction * operator_image), ('group', 'block'))  83.8 us
    unnamed x3, blocking collectives  65.9 us
    dot_general x2, matrix products, on_device(): jnp.einsum('src,sc->sr', got_blocks, inputs, preferred_element_type=jnp.f...  20.3 us
    dot_general x2, matrix products, on_device(): jnp.einsum('src,sr->sc', got_blocks, projected, preferred_element_type=jn...  15.7 us
    ppermute x6, starting transfers between devices, on_device(): v_next.append(ppermute(v_next[-1], axis_name='group', perm=gallery))  15.1 us
  transfers between devices with their start and end apart: 16, of which 9 were waited for; matrix products, arithmetic and copies ran while one was open for 3% of the time, Pallas kernels for 0%

profile of v1, /device:TPU:1, one launch (start us, length us, event | category | flops | bytes accessed | tf_op | source)
XLA Modules:
  0.0 741.3 jit_solution(4823526198756674383)
XLA Ops:
  3.7 8.6 %all-to-all-start = ((s32[32,1,2]{2,1,0:T(1,128)}), s32[32,1,2]{2,1,0:T(1,128)S(1)}, u32[]{:S(2)}, u32[]{:S(2)}) async-start(s32[32,1,2]{2,1,0:T(1,128)} %bitcast.2), calls=%async_computation | async-start | bytes 32768 | tf_op jit(solution)/shard_map/all_to_all | solution.py:40
  13.0 2.3 broadcast_select_fusion
  15.3 7.1 broadcast_in_dim.26
  22.4 7.7 %scatter_fusion = bf16[64,128,1152]{2,1,0:T(8,128)(2,1)} fusion(bf16[64,128,1152]{2,1,0:T(8,128)(2,1)} %broadcast_in_dim.26, s32[12]{0:T(128)} %copy-done.2, bf16[12,128,1152]{2,1,0:T(8,128)(2,1)S(1)} %broadcast_select_fusion), kind=kCustom, calls=%fused_computation.1 | custom fusion | bytes 10616880 | tf_op jit(solution)/shard_map/scatter | solution.py:33
  30.2 7.5 %all-to-all-start.1 = ((bf16[32,2,128,1152]{3,2,1,0:T(8,128)(2,1)}), bf16[32,2,128,1152]{3,2,1,0:T(8,128)(2,1)}, u32[]{:S(2)}, u32[]{:S(2)}) async-start(bf16[32,2,128,1152]{3,2,1,0:T(8,128)(2,1)} %bitcast.31), calls=%async_computation.1 | async-start | bytes 37748736 | tf_op jit(solution)/shard_map/all_to_all | solution.py:39
  39.6 261.2 %all-to-all-done.1 = bf16[32,2,128,1152]{3,2,1,0:T(8,128)(2,1)} async-done(((bf16[32,2,128,1152]{3,2,1,0:T(8,128)(2,1)}), bf16[32,2,128,1152]{3,2,1,0:T(8,128)(2,1)}, u32[]{:S(2)}, u32[]{:S(2)}) %all-to-all-start.1) | async-done | bytes 18874400 | tf_op jit(solution)/shard_map/all_to_all | solution.py:39
  300.8 8.3 %fusion = f32[64,1152]{1,0:T(8,128)S(1)} fusion(bf16[32,2,128,1152]{3,2,1,0:T(8,128)(2,1)} %all-to-all-done.1), kind=kLoop, calls=%fused_computation.3 | loop fusion | flops 28237824 | bytes 19169280 | tf_op jit(solution)/shard_map/src,src->sc/dot_general | solution.py:59
  309.4 25.5 %all-reduce = f32[8,576]{1,0:T(8,128)S(1)} all-reduce(f32[8,576]{1,0:T(8,128)S(1)} %convolution_add_fusion.2), channel_id=2, replica_groups=mesh['group'=8,'block'=32] {'group'}, use_global_device_ids=true, to_apply=%region_4.5.clone | all-reduce | flops 4608 | bytes 36864
  335.7 2.7 collective-permute-start.4
  338.3 1.0 collective-permute-done
  339.3 2.7 collective-permute-start.5
  343.0 2.7 collective-permute-start.6
  346.6 3.6 collective-permute-done.3
  350.6 10.1 %fusion.3 = f32[64,1,128]{2,1,0:T(1,128)S(1)} fusion(bf16[64,128,1152]{2,1,0:T(8,128)(2,1)} %bitcast.4, bf16[64,1152,1]{1,0,2:T(8,128)(2,1)S(1)} %maximum_bitcast_fusion), kind=kOutput, calls=%fused_computation.14 | convolution fusion | flops 18874368 | bytes 19054592 | tf_op jit(solution)/shard_map/src,sc->sr/dot_general | solution.py:91
  360.8 7.8 %fusion.10 = f32[64,1,1152]{2,1,0:T(1,128)S(1)} fusion(bf16[64,128,1152]{2,1,0:T(8,128)(2,1)} %bitcast.4, bf16[64,128,1]{1,0,2:T(8,128)(2,1)S(1)} %convert_bitcast_fusion.1), kind=kOutput, calls=%fused_computation.26 | convolution fusion | flops 18874368 | bytes 19185664 | tf_op jit(solution)/shard_map/src,sr->sc/dot_general | solution.py:94
  369.0 20.1 %all-reduce.1 = f32[8,576]{1,0:T(8,128)S(1)} all-reduce(f32[8,576]{1,0:T(8,128)S(1)} %convolution_add_fusion.1), channel_id=3, replica_groups=mesh['group'=8,'block'=32] {'group'}, use_global_device_ids=true, to_apply=%region_8.10.clone | all-reduce | flops 4608 | bytes 36864
  389.1 1.2 multiply_reduce_fusion.2
  390.3 132.3 %all-reduce.3 = (f32[]{:T(128)}, f32[]{:T(128)}) all-reduce(f32[]{:T(128)} %get-tuple-element.4, f32[]{:T(128)} %get-tuple-element.3), channel_id=1, replica_groups=mesh['group'=8,'block'=32] {'group','block'}, use_global_device_ids=true, to_apply=%region_6.7 | all-reduce | flops 2 | bytes 16 | tf_op jit(solution)/shard_map/psum | solution.py:11
  524.0 1.2 multiply_reduce_fusion.1
  525.2 73.4 %psum.30 = f32[]{:T(128)} all-reduce(f32[]{:T(128)} %get-tuple-element.9), channel_id=1, replica_groups=mesh['group'=8,'block'=32] {'group','block'}, use_global_device_ids=true, to_apply=%region_12.14 | all-reduce | flops 1 | bytes 8 | tf_op jit(solution)/shard_map/psum | solution.py:11
  600.0 1.0 collective-permute-start.7
  601.0 1.8 collective-permute-start.11
  602.8 1.0 collective-permute-done.7
  603.7 2.7 collective-permute-start.12
  607.4 2.7 collective-permute-start.13
  611.1 3.7 collective-permute-done.10
  615.1 10.1 %fusion.1 = f32[64,1,128]{2,1,0:T(1,128)S(1)} fusion(bf16[64,128,1152]{2,1,0:T(8,128)(2,1)} %bitcast.4, bf16[64,1152,1]{1,0,2:T(8,128)(2,1)S(1)} %maximum_bitcast_fusion.1), kind=kOutput, calls=%fused_computation.11 | convolution fusion | flops 18874368 | bytes 19054592 | tf_op jit(solution)/shard_map/src,sc->sr/dot_general | solution.py:91
  625.3 7.8 %fusion.8 = f32[64,1,1152]{2,1,0:T(1,128)S(1)} fusion(bf16[64,128,1152]{2,1,0:T(8,128)(2,1)} %bitcast.4, bf16[64,128,1]{1,0,2:T(8,128)(2,1)S(1)} %convert_bitcast_fusion), kind=kOutput, calls=%fused_computation.24 | convolution fusion | flops 18874368 | bytes 19185664 | tf_op jit(solution)/shard_map/src,sr->sc/dot_general | solution.py:94
  633.4 20.2 %all-reduce.2 = f32[8,576]{1,0:T(8,128)S(1)} all-reduce(f32[8,576]{1,0:T(8,128)S(1)} %convolution_add_fusion), channel_id=4, replica_groups=mesh['group'=8,'block'=32] {'group'}, use_global_device_ids=true, to_apply=%region_14.16.clone | all-reduce | flops 4608 | bytes 36864
  653.7 1.2 multiply_reduce_fusion
  654.9 83.8 %psum.31 = f32[]{:T(128)} all-reduce(f32[]{:T(128)} %multiply_reduce_fusion), channel_id=1, replica_groups=mesh['group'=8,'block'=32] {'group','block'}, use_global_device_ids=true, to_apply=%region_16.18 | all-reduce | flops 1 | bytes 8 | tf_op jit(solution)/shard_map/psum | solution.py:100
  740.1 1.2 multiply_subtract_fusion
  (58 shorter events, 12.0 us)
Async XLA Ops:
  2.2 10.0 %copy-start.2 = (s32[12]{0:T(128)}, s32[12]{0:T(128)S(1)}, u32[]{:S(2)}) copy-start(s32[12]{0:T(128)S(1)} %compare_select_fusion) | copy-start | bytes 148
  3.7 26.5 %all-to-all-start = ((s32[32,1,2]{2,1,0:T(1,128)}), s32[32,1,2]{2,1,0:T(1,128)S(1)}, u32[]{:S(2)}, u32[]{:S(2)}) async-start(s32[32,1,2]{2,1,0:T(1,128)} %bitcast.2), calls=%async_computation | async-start | bytes 32768 | tf_op jit(solution)/shard_map/all_to_all | solution.py:40
  30.2 7.6 %copy-start.3 = (u32[256]{0:T(256)S(1)}, u32[256]{0:T(256)}, u32[]{:S(2)}) copy-start(u32[256]{0:T(256)} %constant.48) | copy-start | bytes 3076
  30.2 270.6 %all-to-all-start.1 = ((bf16[32,2,128,1152]{3,2,1,0:T(8,128)(2,1)}), bf16[32,2,128,1152]{3,2,1,0:T(8,128)(2,1)}, u32[]{:S(2)}, u32[]{:S(2)}) async-start(bf16[32,2,128,1152]{3,2,1,0:T(8,128)(2,1)} %bitcast.31), calls=%async_computation.1 | async-start | bytes 37748736 | tf_op jit(solution)/shard_map/all_to_all | solution.py:39
  37.7 297.2 %copy-start = (f32[1,576]{1,0:T(1,128)S(1)}, f32[1,576]{1,0:T(1,128)}, u32[]{:S(2)}) copy-start(f32[1,576]{1,0:T(1,128)} %param.12) | copy-start | bytes 6916
  37.7 297.2 %copy-start.1 = (f32[1,576]{1,0:T(1,128)S(1)}, f32[1,576]{1,0:T(1,128)}, u32[]{:S(2)}) copy-start(f32[1,576]{1,0:T(1,128)} %param.13) | copy-start | bytes 6916
  335.6 3.7 collective-permute-start
  335.7 3.6 collective-permute-start.4
  339.3 3.7 collective-permute-start.1
  339.3 3.7 collective-permute-start.5
  343.0 3.7 collective-permute-start.2
  343.0 3.7 collective-permute-start.6
  346.6 3.7 collective-permute-start.3
  600.0 3.7 collective-permute-start.7
  601.0 2.8 collective-permute-start.11
  603.7 3.7 collective-permute-start.8
  603.7 3.7 collective-permute-start.12
  607.4 3.7 collective-permute-start.9
  607.4 3.7 collective-permute-start.13
  611.0 3.7 collective-permute-start.10
